TPU v7x, 32 devices: a whole 2x2x4 slice. The times are simulated.
32 devices in a mesh: tm: 4 (over z), ha: 2 (over y), wa: 4 (over x, core).
Axes of the slice: x: 2, y: 2, z: 4, core: 2. Of those that a mesh axis runs over, the one named last changes fastest.
Arguments:
- latent: bfloat16 [8, 32, 64, 512], P('tm', 'ha', 'wa'), may hold values from -1300 to 1300
- norm_gain: float32 [512], replicated, may hold values from 0.1 to 1.9
- norm_bias: float32 [512], replicated, may hold values from -3 to 3
- conv_weight: bfloat16 [3, 3, 3, 512, 256], replicated, may hold values from -0.0546875 to 0.0546875
- conv_bias: float32 [256], replicated, may hold values from -3 to 3
- up_weight: bfloat16 [4, 4, 256, 256], replicated, may hold values from -0.1875 to 0.1875
- up_bias: float32 [256], replicated, may hold values from -3 to 3
Outputs:
- video: bfloat16 [8, 64, 128, 256], P('tm', 'ha', 'wa')
All inputs are finite; a program needn't handle non-finite values.
Results may differ from a plain program's by a relative error of at most 0.0054.
Values may be sent and summed in bfloat16 or wider, within the bound.
A program may use at most 64 MiB of HBM per device.

v0:
```python
import jax
import jax.numpy as jnp
from jax import lax
from jax.sharding import PartitionSpec as P

GROUPS = 32


def prefix(part, axis, combine, identity):
    place = lax.axis_index(axis)
    gathered = jax.tree.map(lambda a: lax.all_gather(a, axis), part)
    state = jax.tree.map(lambda a, e: jnp.zeros_like(a) + jnp.asarray(e, a.dtype), part, identity)

    def one(hop, state):
        return combine(
            state, jax.tree.map(lambda a: lax.dynamic_index_in_dim(a, hop, 0, False), gathered)
        )

    return lax.fori_loop(0, place, one, state)


def padded_2(block, sides, width):
    for axis, dim in sides:
        count = lax.axis_size(axis)
        forward = [(i, i + 1) for i in range(count - 1)]
        backward = [(target, source) for source, target in forward]
        low = lax.ppermute(
            lax.slice_in_dim(block, block.shape[dim] - width, None, axis=dim), axis, forward
        )
        high = lax.ppermute(lax.slice_in_dim(block, 0, width, axis=dim), axis, backward)
        block = jnp.concatenate([low, block, high], axis=dim)
    return block


def from_behind(array, axis, by):
    devices = lax.axis_size(axis)
    pairs = [(i, i + by) for i in range(devices) if 0 <= i + by < devices]
    return lax.ppermute(array, axis, pairs)


def group_totals(latent):
    wide = latent.astype(jnp.float32)
    sums = jnp.sum(wide, axis=(0, 1, 2)).reshape(GROUPS, -1).sum(axis=1)
    squares = jnp.sum(wide * wide, axis=(0, 1, 2)).reshape(GROUPS, -1).sum(axis=1)
    return (sums, squares)


def add_pair(earlier, later):
    return (earlier[0] + later[0], earlier[1] + later[1])


def tap_sum(source, weights, height, breadth):
    count = source.shape[0]
    summed = None
    for row_tap in range(3):
        joined = jnp.concatenate(
            [
                source[:, row_tap : row_tap + height, col_tap : col_tap + breadth, :]
                for col_tap in range(3)
            ],
            axis=-1,
        )
        joined = joined.reshape(count * height * breadth, -1)
        term = jnp.dot(
            joined,
            weights[row_tap].reshape(-1, weights.shape[-1]),
            preferred_element_type=jnp.float32,
        )
        summed = term if summed is None else summed + term
    return summed


def upsample_tile(values, up_weight):
    frames, height, breadth, chans = values.shape
    flat = values.reshape(frames * height * breadth, chans)
    rows_out = []
    for row_par in (0, 1):
        cols_out = []
        for col_par in (0, 1):
            joined = jnp.concatenate(
                [
                    up_weight[row_par + 2 * shift_row, col_par + 2 * shift_col]
                    for shift_row in (0, 1)
                    for shift_col in (0, 1)
                ],
                axis=1,
            )
            product = jnp.dot(flat, joined, preferred_element_type=jnp.float32).reshape(
                frames, height, breadth, 4, chans
            )
            summed = jnp.zeros((frames, height + 1, breadth + 1, chans), jnp.float32)
            for shift_row in (0, 1):
                for shift_col in (0, 1):
                    summed = summed + jnp.pad(
                        product[:, :, :, 2 * shift_row + shift_col],
                        ((0, 0), (shift_row, 1 - shift_row), (shift_col, 1 - shift_col), (0, 0)),
                    )
            cols_out.append(summed)
        rows_out.append(jnp.stack(cols_out, axis=3))
    return jnp.stack(rows_out, axis=2).reshape(frames, 2 * height + 2, 2 * breadth + 2, chans)


def shards(latent, norm_gain, norm_bias, conv_weight, conv_bias, up_weight, up_bias):
    frames, height, breadth, channels = latent.shape
    block_index = lax.axis_index("tm")
    tile_sums, tile_squares = group_totals(latent)
    block_sums, block_squares = lax.psum((tile_sums, tile_squares), ("ha", "wa"))
    zeros_pair = (jnp.zeros_like(block_sums), jnp.zeros_like(block_squares))
    before = prefix((block_sums, block_squares), "tm", add_pair, zeros_pair)
    upto_sums = before[0] + block_sums
    upto_squares = before[1] + block_squares
    group_width = channels // GROUPS
    cells = float(
        frames * height * breadth * lax.axis_size("ha") * lax.axis_size("wa") * group_width
    )
    counted = (block_index + 1).astype(jnp.float32) * cells
    mean = upto_sums / counted
    variance = upto_squares / counted - mean * mean
    inverse = lax.rsqrt(variance + 1e-06)
    mean_chan = jnp.repeat(mean, group_width)
    inverse_chan = jnp.repeat(inverse, group_width)
    normed = jax.nn.silu(
        (latent.astype(jnp.float32) - mean_chan) * inverse_chan * norm_gain + norm_bias
    ).astype(jnp.bfloat16)
    padded = padded_2(normed, (("ha", 1), ("wa", 2)), 1)
    earlier = from_behind(padded, "tm", 1)
    opening = jnp.stack([padded[0], padded[0]])
    earlier = jnp.where(block_index == 0, opening, earlier)
    extended = jnp.concatenate([earlier, padded], axis=0)
    summed = None
    for lag_step in range(3):
        term = tap_sum(
            extended[lag_step : lag_step + frames], conv_weight[lag_step], height, breadth
        )
        summed = term if summed is None else summed + term
    features = (summed + conv_bias).astype(jnp.bfloat16).reshape(frames, height, breadth, -1)
    spread = upsample_tile(features, up_weight)
    from_above = from_behind(spread[:, -1].astype(jnp.bfloat16), "ha", 1).astype(jnp.float32)
    from_below = from_behind(spread[:, 0].astype(jnp.bfloat16), "ha", -1).astype(jnp.float32)
    middle = spread[:, 1:-1]
    middle = middle.at[:, 0].add(from_above)
    middle = middle.at[:, -1].add(from_below)
    from_left = from_behind(middle[:, :, -1].astype(jnp.bfloat16), "wa", 1).astype(jnp.float32)
    from_right = from_behind(middle[:, :, 0].astype(jnp.bfloat16), "wa", -1).astype(jnp.float32)
    inner = middle[:, :, 1:-1]
    inner = inner.at[:, :, 0].add(from_left)
    inner = inner.at[:, :, -1].add(from_right)
    return (inner + up_bias).astype(jnp.bfloat16)


def solution(mesh):
    in_specs = (P("tm", "ha", "wa", None), P(), P(), P(), P(), P(), P())
    out_specs = P("tm", "ha", "wa", None)
    return jax.shard_map(shards, mesh=mesh, in_specs=in_specs, out_specs=out_specs, check_vma=False)
```

profile of v0, /device:TPU:9, one launch (start us, length us, event | category | flops | bytes accessed | tf_op | source)
XLA Modules:
  0.0 143.2 jit_solution(13787219909280827165)
XLA Ops:
  0.0 1.2 fusion.9
  1.6 11.8 %all-reduce.18 = (f32[32]{0:T(128)S(1)}, f32[32]{0:T(128)S(1)}) all-reduce(f32[32]{0:T(128)S(1)} %reduce_sum.37, f32[32]{0:T(128)S(1)} %reduce_sum.39), channel_id=1, replica_groups=mesh['tm'=4,'ha'=2,'wa'=4] {'ha','wa'}, use_global_device_ids=true, to_apply=%region_2.0 | all-reduce | flops 64 | bytes 512 | tf_op jit(solution)/shard_map/psum | solution.py:107
  13.4 1.2 dynamic-slice.32
  15.7 6.9 %all-reduce.19 = (f32[128]{0:T(128)S(1)}, f32[128]{0:T(128)S(1)}) all-reduce(f32[128]{0:T(128)S(1)} %dynamic-update-slice.12, f32[128]{0:T(128)S(1)} %dynamic-update-slice.13), channel_id=2, replica_groups=mesh['tm'=4,'ha'=2,'wa'=4] {'tm'}, use_global_device_ids=true, to_apply=%add.16 | all-reduce | flops 256 | bytes 2048
  23.1 1.4 %fusion.18 = bf16[2,16,16,512]{3,2,1,0:T(8,128)(2,1)S(1)} fusion(bf16[2,16,16,512]{3,2,1,0:T(8,128)(2,1)} %param.17, f32[512]{0:T(512)} %param.19, f32[512]{0:T(512)} %param.18, f32[512]{0:T(512)S(1)} %mul.34, f32[512]{0:T(512)S(1)} %sub.13), kind=kLoop, calls=%fused_computation.42 | loop fusion | flops 2621440 | bytes 1056768 | tf_op jit(solution)/shard_map/convert_element_type | solution.py:124
  24.6 1.3 collective-permute-start.1
  25.9 4.0 %collective-permute-start = (bf16[2,1,16,512]{3,2,1,0:T(8,128)(2,1)S(1)}, bf16[2,1,16,512]{3,2,1,0:T(8,128)(2,1)S(1)}, u32[]{:S(2)}, u32[]{:S(2)}) collective-permute-start(bf16[2,1,16,512]{3,2,1,0:T(8,128)(2,1)S(1)} %get-tuple-element.187), channel_id=1, source_target_pairs={{0,4},{1,5},{2,6},{3,7},{8,12},{9,13},{10,14},{11,15},{16,20},{17,... | collective-permute-start | bytes 98312 | tf_op jit(solution)/shard_map/ppermute | solution.py:27
  29.9 5.9 %fusion.58 = (bf16[1,1,3,512,256]{4,3,2,1,0:T(8,128)(2,1)S(1)}, bf16[1,1,3,512,256]{4,3,2,1,0:T(8,128)(2,1)}, bf16[1,1,3,512,256]{4,3,2,1,0:T(8,128)(2,1)}, bf16...) fusion(bf16[3,3,3,512,256]{4,3,2,1,0:T(8,128)(2,1)} %param.20), kind=kLoop, calls=%fused_computation.136 | loop fusion | bytes 14155776 | tf_op jit(solution)/shard_map/slice | solution.py:66
  36.0 7.0 %collective-permute-start.3 = (bf16[2,18,1,512]{3,2,1,0:T(2,128)(2,1)S(1)}, bf16[2,18,1,512]{3,2,1,0:T(2,128)(2,1)S(1)}, u32[]{:S(2)}, u32[]{:S(2)}) collective-permute-start(bf16[2,18,1,512]{3,2,1,0:T(2,128)(2,1)S(1)} %get-tuple-element.183), channel_id=1, source_target_pairs={{1,0},{2,1},{3,2},{5,4},{6,5},{7,6},{9,8},{10,9},{11,10},{13,12},{... | collective-permute-start | bytes 110600 | tf_op jit(solution)/shard_map/ppermute | solution.py:30
  43.0 1.9 %collective-permute-start.2 = (bf16[2,18,1,512]{3,2,1,0:T(2,128)(2,1)S(1)}, bf16[2,18,1,512]{3,2,1,0:T(2,128)(2,1)S(1)}, u32[]{:S(2)}, u32[]{:S(2)}) collective-permute-start(bf16[2,18,1,512]{3,2,1,0:T(2,128)(2,1)S(1)} %get-tuple-element.182), channel_id=1, source_target_pairs={{0,1},{1,2},{2,3},{4,5},{5,6},{6,7},{8,9},{9,10},{10,11},{12,13},{... | collective-permute-start | bytes 110600 | tf_op jit(solution)/shard_map/ppermute | solution.py:27
  46.8 3.2 %collective-permute-start.4 = (bf16[2,18,18,512]{3,2,1,0:T(8,128)(2,1)S(1)}, bf16[2,18,18,512]{3,2,1,0:T(8,128)(2,1)S(1)}, u32[]{:S(2)}, u32[]{:S(2)}) collective-permute-start(bf16[2,18,18,512]{3,2,1,0:T(8,128)(2,1)S(1)} %pad_maximum_fusion.10), channel_id=1, source_target_pairs={{0,8},{8,16},{16,24},{1,9},{9,17},{17,25},{2,10},{10,18},{18,26},{... | collective-permute-start | bytes 1990664 | tf_op jit(solution)/shard_map/ppermute | solution.py:38
  53.4 17.6 %collective-permute-done.4 = bf16[2,18,18,512]{3,2,1,0:T(8,128)(2,1)S(1)} collective-permute-done((bf16[2,18,18,512]{3,2,1,0:T(8,128)(2,1)S(1)}, bf16[2,18,18,512]{3,2,1,0:T(8,128)(2,1)S(1)}, u32[]{:S(2)}, u32[]{:S(2)}) %collective-permute-start.4) | collective-permute-done | bytes 663584 | tf_op jit(solution)/shard_map/ppermute | solution.py:38
  82.2 1.8 %fusion.43 = f32[512,1024]{1,0:T(8,128)} fusion(bf16[512,256]{1,0:T(8,128)(2,1)S(1)} %fusion.8, bf16[256,256]{1,0:T(8,128)(2,1)S(1)} %copy-done.30, bf16[256,256]{1,0:T(8,128)(2,1)S(1)} %copy-done.31, bf16[256,256]{1,0:T(8,128)(2,1)S(1)} %get-tuple-element.125, bf16[256,256]{1,0:T(8,128)(2,1)S(1)} %get-tuple-element.126), kind=kOutput, calls=%fused_computation.75 | convolution fusion | flops 270532608 | bytes 2883584 | tf_op jit(solution)/shard_map/dot_general | solution.py:88
  84.0 2.2 %reshape.235 = f32[2,16,16,4,256]{4,3,2,1,0:T(4,128)S(1)} reshape(f32[512,1024]{1,0:T(8,128)} %fusion.43) | data formatting | bytes 4194304 | tf_op jit(solution)/shard_map/reshape | solution.py:88
  86.2 1.9 %fusion.62 = (f32[2,16,16,1,256]{4,3,2,1,0:T(1,128)S(1)}, f32[2,16,16,1,256]{4,3,2,1,0:T(1,128)S(1)}, f32[2,16,16,1,256]{4,3,2,1,0:T(1,128)S(1)}, f32[2,16,16,1,256]{4,3,2,1,0:T(1,128)S(1)}) fusion(f32[2,16,16,4,256]{4,3,2,1,0:T(4,128)S(1)} %reshape.235), kind=kLoop, calls=%fused_computation.140 | loop fusion | bytes 4194304 | tf_op jit(solution)/shard_map/slice | solution.py:95
  89.9 1.8 %fusion.35 = f32[512,1024]{1,0:T(8,128)} fusion(bf16[512,256]{1,0:T(8,128)(2,1)S(1)} %fusion.8, bf16[256,256]{1,0:T(8,128)(2,1)S(1)} %copy-done.26, bf16[256,256]{1,0:T(8,128)(2,1)S(1)} %copy-done.27, bf16[256,256]{1,0:T(8,128)(2,1)S(1)} %copy-done.28, bf16[256,256]{1,0:T(8,128)(2,1)S(1)} %copy-done.29), kind=kOutput, calls=%fused_computation.67 | convolution fusion | flops 270532608 | bytes 2883584 | tf_op jit(solution)/shard_map/dot_general | solution.py:88
  91.7 2.2 %reshape.234 = f32[2,16,16,4,256]{4,3,2,1,0:T(4,128)S(1)} reshape(f32[512,1024]{1,0:T(8,128)} %fusion.35) | data formatting | bytes 4194304 | tf_op jit(solution)/shard_map/reshape | solution.py:88
  93.9 1.9 %fusion.61 = (f32[2,16,16,1,256]{4,3,2,1,0:T(1,128)S(1)}, f32[2,16,16,1,256]{4,3,2,1,0:T(1,128)S(1)}, f32[2,16,16,1,256]{4,3,2,1,0:T(1,128)S(1)}, f32[2,16,16,1,256]{4,3,2,1,0:T(1,128)S(1)}) fusion(f32[2,16,16,4,256]{4,3,2,1,0:T(4,128)S(1)} %reshape.234), kind=kLoop, calls=%fused_computation.139 | loop fusion | bytes 4194304 | tf_op jit(solution)/shard_map/slice | solution.py:95
  99.2 1.8 %fusion.27 = f32[512,1024]{1,0:T(8,128)} fusion(bf16[512,256]{1,0:T(8,128)(2,1)S(1)} %fusion.8, bf16[256,256]{1,0:T(8,128)(2,1)S(1)} %copy-done.22, bf16[256,256]{1,0:T(8,128)(2,1)S(1)} %copy-done.23, bf16[256,256]{1,0:T(8,128)(2,1)S(1)} %copy-done.24, bf16[256,256]{1,0:T(8,128)(2,1)S(1)} %copy-done.25), kind=kOutput, calls=%fused_computation.59 | convolution fusion | flops 270532608 | bytes 2883584 | tf_op jit(solution)/shard_map/dot_general | solution.py:88
  101.0 2.2 %reshape.233 = f32[2,16,16,4,256]{4,3,2,1,0:T(4,128)S(1)} reshape(f32[512,1024]{1,0:T(8,128)} %fusion.27) | data formatting | bytes 4194304 | tf_op jit(solution)/shard_map/reshape | solution.py:88
  103.2 1.9 %fusion.60 = (f32[2,16,16,1,256]{4,3,2,1,0:T(1,128)S(1)}, f32[2,16,16,1,256]{4,3,2,1,0:T(1,128)S(1)}, f32[2,16,16,1,256]{4,3,2,1,0:T(1,128)S(1)}, f32[2,16,16,1,256]{4,3,2,1,0:T(1,128)S(1)}) fusion(f32[2,16,16,4,256]{4,3,2,1,0:T(4,128)S(1)} %reshape.233), kind=kLoop, calls=%fused_computation.138 | loop fusion | bytes 4194304 | tf_op jit(solution)/shard_map/slice | solution.py:95
  108.9 2.0 %reshape.232 = f32[2,16,16,4,256]{4,3,2,1,0:T(4,128)} reshape(f32[512,1024]{1,0:T(8,128)S(1)} %fusion.19) | data formatting | bytes 4194304 | tf_op jit(solution)/shard_map/reshape | solution.py:88
  111.0 5.9 %fusion.59 = (f32[2,16,16,1,256]{4,3,2,1,0:T(1,128)S(1)}, f32[2,16,16,1,256]{4,3,2,1,0:T(1,128)S(1)}, f32[2,16,16,1,256]{4,3,2,1,0:T(1,128)S(1)}, f32[2,16,16,1,256]{4,3,2,1,0:T(1,128)S(1)}) fusion(f32[2,16,16,4,256]{4,3,2,1,0:T(4,128)} %reshape.232), kind=kLoop, calls=%fused_computation.137 | loop fusion | bytes 4194304 | tf_op jit(solution)/shard_map/slice | solution.py:95
  121.6 1.2 copy.43
  123.7 1.3 collective-permute-start.5
  125.8 1.3 collective-permute-start.6
  127.6 2.9 %collective-permute-done.6 = bf16[2,34,256]{2,0,1:T(2,128)(2,1)S(1)} collective-permute-done((bf16[2,34,256]{2,0,1:T(2,128)(2,1)S(1)}, bf16[2,34,256]{2,0,1:T(2,128)(2,1)S(1)}, u32[]{:S(2)}, u32[]{:S(2)}) %collective-permute-start.6) | collective-permute-done | bytes 34848 | tf_op jit(solution)/shard_map/ppermute | solution.py:38
  130.6 2.8 %scatter-add.15 = f32[2,32,34,256]{3,1,0,2:T(8,128)S(1)} dynamic-update-slice(f32[2,32,34,256]{3,1,0,2:T(8,128)S(1)} %copy.45, f32[2,1,34,256]{3,1,0,2:T(1,128)S(1)} %copy_add_fusion, s32[]{:T(128)} %constant.128.clone.1, s32[]{:T(128)} %constant.134.clone.1, s32[]{:T(128)} %constant.128.clone.1, s32[]{:T(128)} %constant.128.clone.1) | dynamic-update-slice | bytes 139268 | tf_op jit(solution)/shard_map/scatter-add | solution.py:142
  133.7 2.2 %collective-permute-start.7 = (bf16[2,32,256]{2,1,0:T(8,128)(2,1)S(1)}, bf16[2,32,256]{2,1,0:T(8,128)(2,1)S(1)}, u32[]{:S(2)}, u32[]{:S(2)}) collective-permute-start(bf16[2,32,256]{2,1,0:T(8,128)(2,1)S(1)} %get-tuple-element.164), channel_id=1, source_target_pairs={{0,1},{1,2},{2,3},{4,5},{5,6},{6,7},{8,9},{9,10},{10,11},{12,13},{... | collective-permute-start | bytes 98312 | tf_op jit(solution)/shard_map/ppermute | solution.py:38
  136.0 3.0 %collective-permute-start.8 = (bf16[2,32,256]{2,1,0:T(8,128)(2,1)S(1)}, bf16[2,32,256]{2,1,0:T(8,128)(2,1)S(1)}, u32[]{:S(2)}, u32[]{:S(2)}) collective-permute-start(bf16[2,32,256]{2,1,0:T(8,128)(2,1)S(1)} %get-tuple-element.163), channel_id=1, source_target_pairs={{1,0},{2,1},{3,2},{5,4},{6,5},{7,6},{9,8},{10,9},{11,10},{13,12},{... | collective-permute-start | bytes 98312 | tf_op jit(solution)/shard_map/ppermute | solution.py:38
  139.1 2.2 %collective-permute-done.8 = bf16[2,32,256]{2,1,0:T(8,128)(2,1)S(1)} collective-permute-done((bf16[2,32,256]{2,1,0:T(8,128)(2,1)S(1)}, bf16[2,32,256]{2,1,0:T(8,128)(2,1)S(1)}, u32[]{:S(2)}, u32[]{:S(2)}) %collective-permute-start.8) | collective-permute-done | bytes 32800 | tf_op jit(solution)/shard_map/ppermute | solution.py:38
  141.6 1.6 %copy.46 = bf16[2,32,32,256]{3,2,1,0:T(8,128)(2,1)} copy(bf16[2,32,32,256]{3,1,0,2:T(8,128)(2,1)S(1)} %add_convert_fusion) | data formatting | bytes 2097152 | tf_op jit(solution)/shard_map/convert_element_type | solution.py:148
  (156 shorter events, 34.0 us)
Async XLA Ops:
  24.6 11.3 %collective-permute-start.1 = (bf16[2,1,16,512]{3,2,1,0:T(8,128)(2,1)S(1)}, bf16[2,1,16,512]{3,2,1,0:T(8,128)(2,1)S(1)}, u32[]{:S(2)}, u32[]{:S(2)}) collective-permute-start(bf16[2,1,16,512]{3,2,1,0:T(8,128)(2,1)S(1)} %get-tuple-element.188), channel_id=1, source_target_pairs={{4,0},{5,1},{6,2},{7,3},{12,8},{13,9},{14,10},{15,11},{20,16},{21,... | collective-permute-start | bytes 98312 | tf_op jit(solution)/shard_map/ppermute | solution.py:30
  25.9 10.0 %collective-permute-start = (bf16[2,1,16,512]{3,2,1,0:T(8,128)(2,1)S(1)}, bf16[2,1,16,512]{3,2,1,0:T(8,128)(2,1)S(1)}, u32[]{:S(2)}, u32[]{:S(2)}) collective-permute-start(bf16[2,1,16,512]{3,2,1,0:T(8,128)(2,1)S(1)} %get-tuple-element.187), channel_id=1, source_target_pairs={{0,4},{1,5},{2,6},{3,7},{8,12},{9,13},{10,14},{11,15},{16,20},{17,... | collective-permute-start | bytes 98312 | tf_op jit(solution)/shard_map/ppermute | solution.py:27
  29.9 15.0 %copy-start.8 = (bf16[4,4,256,256]{3,2,1,0:T(8,128)(2,1)S(1)}, bf16[4,4,256,256]{3,2,1,0:T(8,128)(2,1)}, u32[]{:S(2)}) copy-start(bf16[4,4,256,256]{3,2,1,0:T(8,128)(2,1)} %param.22) | copy-start | bytes 6291460
  36.0 10.2 %collective-permute-start.3 = (bf16[2,18,1,512]{3,2,1,0:T(2,128)(2,1)S(1)}, bf16[2,18,1,512]{3,2,1,0:T(2,128)(2,1)S(1)}, u32[]{:S(2)}, u32[]{:S(2)}) collective-permute-start(bf16[2,18,1,512]{3,2,1,0:T(2,128)(2,1)S(1)} %get-tuple-element.183), channel_id=1, source_target_pairs={{1,0},{2,1},{3,2},{5,4},{6,5},{7,6},{9,8},{10,9},{11,10},{13,12},{... | collective-permute-start | bytes 110600 | tf_op jit(solution)/shard_map/ppermute | solution.py:30
  43.0 3.3 %collective-permute-start.2 = (bf16[2,18,1,512]{3,2,1,0:T(2,128)(2,1)S(1)}, bf16[2,18,1,512]{3,2,1,0:T(2,128)(2,1)S(1)}, u32[]{:S(2)}, u32[]{:S(2)}) collective-permute-start(bf16[2,18,1,512]{3,2,1,0:T(2,128)(2,1)S(1)} %get-tuple-element.182), channel_id=1, source_target_pairs={{0,1},{1,2},{2,3},{4,5},{5,6},{6,7},{8,9},{9,10},{10,11},{12,13},{... | collective-permute-start | bytes 110600 | tf_op jit(solution)/shard_map/ppermute | solution.py:27
  46.8 24.2 %collective-permute-start.4 = (bf16[2,18,18,512]{3,2,1,0:T(8,128)(2,1)S(1)}, bf16[2,18,18,512]{3,2,1,0:T(8,128)(2,1)S(1)}, u32[]{:S(2)}, u32[]{:S(2)}) collective-permute-start(bf16[2,18,18,512]{3,2,1,0:T(8,128)(2,1)S(1)} %pad_maximum_fusion.10), channel_id=1, source_target_pairs={{0,8},{8,16},{16,24},{1,9},{9,17},{17,25},{2,10},{10,18},{18,26},{... | collective-permute-start | bytes 1990664 | tf_op jit(solution)/shard_map/ppermute | solution.py:38
  51.6 1.2 copy-start.2
  75.1 1.4 copy-start.7
  77.2 1.6 %copy-start.5 = (bf16[1,1,3,512,256]{4,3,2,1,0:T(8,128)(2,1)S(1)}, bf16[1,1,3,512,256]{4,3,2,1,0:T(8,128)(2,1)}, u32[]{:S(2)}) copy-start(bf16[1,1,3,512,256]{4,3,2,1,0:T(8,128)(2,1)} %get-tuple-element.114) | copy-start | bytes 2359300
  88.1 1.8 %copy-start.26 = (bf16[256,256]{1,0:T(8,128)(2,1)S(1)}, bf16[256,256]{1,0:T(8,128)(2,1)}, u32[]{:S(2)}) copy-start(bf16[256,256]{1,0:T(8,128)(2,1)} %get-tuple-element.127) | copy-start | bytes 393220
  88.1 1.8 %copy-start.27 = (bf16[256,256]{1,0:T(8,128)(2,1)S(1)}, bf16[256,256]{1,0:T(8,128)(2,1)}, u32[]{:S(2)}) copy-start(bf16[256,256]{1,0:T(8,128)(2,1)} %get-tuple-element.128) | copy-start | bytes 393220
  88.2 1.7 %copy-start.28 = (bf16[256,256]{1,0:T(8,128)(2,1)S(1)}, bf16[256,256]{1,0:T(8,128)(2,1)}, u32[]{:S(2)}) copy-start(bf16[256,256]{1,0:T(8,128)(2,1)} %get-tuple-element.129) | copy-start | bytes 393220
  88.2 1.7 %copy-start.29 = (bf16[256,256]{1,0:T(8,128)(2,1)S(1)}, bf16[256,256]{1,0:T(8,128)(2,1)}, u32[]{:S(2)}) copy-start(bf16[256,256]{1,0:T(8,128)(2,1)} %get-tuple-element.130) | copy-start | bytes 393220
  96.7 2.5 %copy-start.22 = (bf16[256,256]{1,0:T(8,128)(2,1)S(1)}, bf16[256,256]{1,0:T(8,128)(2,1)}, u32[]{:S(2)}) copy-start(bf16[256,256]{1,0:T(8,128)(2,1)} %get-tuple-element.131) | copy-start | bytes 393220
  96.7 2.5 %copy-start.23 = (bf16[256,256]{1,0:T(8,128)(2,1)S(1)}, bf16[256,256]{1,0:T(8,128)(2,1)}, u32[]{:S(2)}) copy-start(bf16[256,256]{1,0:T(8,128)(2,1)} %get-tuple-element.132) | copy-start | bytes 393220
  96.7 2.5 %copy-start.24 = (bf16[256,256]{1,0:T(8,128)(2,1)S(1)}, bf16[256,256]{1,0:T(8,128)(2,1)}, u32[]{:S(2)}) copy-start(bf16[256,256]{1,0:T(8,128)(2,1)} %get-tuple-element.133) | copy-start | bytes 393220
  96.7 2.5 %copy-start.25 = (bf16[256,256]{1,0:T(8,128)(2,1)S(1)}, bf16[256,256]{1,0:T(8,128)(2,1)}, u32[]{:S(2)}) copy-start(bf16[256,256]{1,0:T(8,128)(2,1)} %get-tuple-element.134) | copy-start | bytes 393220
  106.0 2.5 %copy-start.19 = (bf16[256,256]{1,0:T(8,128)(2,1)S(1)}, bf16[256,256]{1,0:T(8,128)(2,1)}, u32[]{:S(2)}) copy-start(bf16[256,256]{1,0:T(8,128)(2,1)} %get-tuple-element.135) | copy-start | bytes 393220
  106.0 2.5 %copy-start.20 = (bf16[256,256]{1,0:T(8,128)(2,1)S(1)}, bf16[256,256]{1,0:T(8,128)(2,1)}, u32[]{:S(2)}) copy-start(bf16[256,256]{1,0:T(8,128)(2,1)} %get-tuple-element.136) | copy-start | bytes 393220
  106.0 2.5 %copy-start.21 = (bf16[256,256]{1,0:T(8,128)(2,1)S(1)}, bf16[256,256]{1,0:T(8,128)(2,1)}, u32[]{:S(2)}) copy-start(bf16[256,256]{1,0:T(8,128)(2,1)} %get-tuple-element.137) | copy-start | bytes 393220
  116.9 1.2 copy-start.10
  117.0 1.4 copy-start.11
  117.0 1.4 copy-start.12
  117.0 1.6 %copy-start.13 = (f32[2,16,16,1,256]{4,2,1,0,3:T(8,128)S(1)}, f32[2,16,16,1,256]{4,2,1,0,3:T(8,128)}, u32[]{:S(2)}) copy-start(f32[2,16,16,1,256]{4,2,1,0,3:T(8,128)} %copy.86) | copy-start | bytes 1572868
  117.0 1.7 %copy-start.14 = (f32[2,16,16,1,256]{4,2,1,0,3:T(8,128)S(1)}, f32[2,16,16,1,256]{4,2,1,0,3:T(8,128)}, u32[]{:S(2)}) copy-start(f32[2,16,16,1,256]{4,2,1,0,3:T(8,128)} %copy.87) | copy-start | bytes 1572868
  119.1 1.3 copy-start.17
  119.1 1.5 %copy-start.18 = (f32[2,16,16,1,256]{4,2,1,0,3:T(8,128)S(1)}, f32[2,16,16,1,256]{4,2,1,0,3:T(8,128)}, u32[]{:S(2)}) copy-start(f32[2,16,16,1,256]{4,2,1,0,3:T(8,128)} %copy.91) | copy-start | bytes 1572868
  123.7 3.4 %collective-permute-start.5 = (bf16[2,34,256]{2,0,1:T(2,128)(2,1)S(1)}, bf16[2,34,256]{2,0,1:T(2,128)(2,1)S(1)}, u32[]{:S(2)}, u32[]{:S(2)}) collective-permute-start(bf16[2,34,256]{2,0,1:T(2,128)(2,1)S(1)} %get-tuple-element.162), channel_id=1, source_target_pairs={{0,4},{1,5},{2,6},{3,7},{8,12},{9,13},{10,14},{11,15},{16,20},{17,... | collective-permute-start | bytes 104456 | tf_op jit(solution)/shard_map/ppermute | solution.py:38
  125.8 4.7 %collective-permute-start.6 = (bf16[2,34,256]{2,0,1:T(2,128)(2,1)S(1)}, bf16[2,34,256]{2,0,1:T(2,128)(2,1)S(1)}, u32[]{:S(2)}, u32[]{:S(2)}) collective-permute-start(bf16[2,34,256]{2,0,1:T(2,128)(2,1)S(1)} %get-tuple-element.161), channel_id=1, source_target_pairs={{4,0},{5,1},{6,2},{7,3},{12,8},{13,9},{14,10},{15,11},{20,16},{21,... | collective-permute-start | bytes 104456 | tf_op jit(solution)/shard_map/ppermute | solution.py:38
  133.7 7.6 %copy-start.33 = (f32[256]{0:T(256)S(1)}, f32[256]{0:T(256)}, u32[]{:S(2)}) copy-start(f32[256]{0:T(256)} %param.23) | copy-start | bytes 3076
  133.7 5.3 %collective-permute-start.7 = (bf16[2,32,256]{2,1,0:T(8,128)(2,1)S(1)}, bf16[2,32,256]{2,1,0:T(8,128)(2,1)S(1)}, u32[]{:S(2)}, u32[]{:S(2)}) collective-permute-start(bf16[2,32,256]{2,1,0:T(8,128)(2,1)S(1)} %get-tuple-element.164), channel_id=1, source_target_pairs={{0,1},{1,2},{2,3},{4,5},{5,6},{6,7},{8,9},{9,10},{10,11},{12,13},{... | collective-permute-start | bytes 98312 | tf_op jit(solution)/shard_map/ppermute | solution.py:38
  136.0 5.2 %collective-permute-start.8 = (bf16[2,32,256]{2,1,0:T(8,128)(2,1)S(1)}, bf16[2,32,256]{2,1,0:T(8,128)(2,1)S(1)}, u32[]{:S(2)}, u32[]{:S(2)}) collective-permute-start(bf16[2,32,256]{2,1,0:T(8,128)(2,1)S(1)} %get-tuple-element.163), channel_id=1, source_target_pairs={{1,0},{2,1},{3,2},{5,4},{6,5},{7,6},{9,8},{10,9},{11,10},{13,12},{... | collective-permute-start | bytes 98312 | tf_op jit(solution)/shard_map/ppermute | solution.py:38
  (11 other events, 11.5 us)
where the time goes:
time: 144 us; the launch traced here: 143 us
  local copies, waits for them, and re-layouts  54.6 us (38%)
  starting transfers between devices  25.2 us (18%)
  waiting for transfers between devices  22.9 us (16%)
  blocking collectives  18.8 us (13%)
  matrix products  10.9 us (8%)
  other arithmetic  9.36 us (6%)
    ppermute x5, waiting for transfers between devices, from_behind(): return lax.ppermute(array, axis, pairs)  22.7 us
    unnamed x89, local copies, waits for them, and re-layouts  17.8 us
    psum x1, blocking collectives, shards(): lax.psum((tile_sums, tile_squares), ('ha', 'wa'))  11.8 us
    slice x4, local copies, waits for them, and re-layouts, upsample_tile(): product[:, :, :, 2 * shift_row + shift_col]  11.6 us
    ppermute x5, starting transfers between devices, from_behind(): return lax.ppermute(array, axis, pairs)  11 us
    reshape x4, local copies, waits for them, and re-layouts, upsample_tile(): jnp.dot(flat, joined, preferred_element_type=jnp.float32)  8.62 us
    ppermute x2, starting transfers between devices, padded_2(): lax.ppermute(lax.slice_in_dim(block, 0, width, axis=dim), axis, backward)  8.3 us
    unnamed x1, blocking collectives  6.94 us
  transfers between devices with their start and end apart: 9, of which 4 were waited for; matrix products, arithmetic and copies ran while one was open for 8% of the time, Pallas kernels for 0%

commit v1 on v0

--- a/solution.py
+++ b/solution.py
@@ -104,7 +104,8 @@
     frames, height, breadth, channels = latent.shape
     block_index = lax.axis_index("tm")
     tile_sums, tile_squares = group_totals(latent)
-    block_sums, block_squares = lax.psum((tile_sums, tile_squares), ("ha", "wa"))
+    balance_the_grid = lambda sample: lax.psum(lax.psum(sample, axis_name="wa"), axis_name="ha")
+    block_sums, block_squares = balance_the_grid((tile_sums, tile_squares))
     zeros_pair = (jnp.zeros_like(block_sums), jnp.zeros_like(block_squares))
     before = prefix((block_sums, block_squares), "tm", add_pair, zeros_pair)
     upto_sums = before[0] + block_sums

time: 144 us -> 144 us (level)
  blocking collectives: 18.8 us -> 16.4 us
    psum x1 -> x2, blocking collectives: 11.8 us -> 9.47 us  [the longest x1 5.69 us: shards(): lax.psum(sample, axis_name='wa')]
where the time goes in v1:
time: 144 us; the launch traced here: 143 us
  local copies, waits for them, and re-layouts  54.6 us (38%)
  starting transfers between devices  26.2 us (18%)
  waiting for transfers between devices  24.1 us (17%)
  blocking collectives  16.4 us (11%)
  matrix products  10.9 us (8%)
  other arithmetic  9.36 us (6%)
    ppermute x5, waiting for transfers between devices, from_behind(): return lax.ppermute(array, axis, pairs)  23.9 us
    unnamed x89, local copies, waits for them, and re-layouts  17.8 us
    slice x4, local copies, waits for them, and re-layouts, upsample_tile(): product[:, :, :, 2 * shift_row + shift_col]  11.7 us
    ppermute x5, starting transfers between devices, from_behind(): return lax.ppermute(array, axis, pairs)  11.4 us
    ppermute x2, starting transfers between devices, padded_2(): lax.ppermute(lax.slice_in_dim(block, 0, width, axis=dim), axis, backward)  8.81 us
    reshape x4, local copies, waits for them, and re-layouts, upsample_tile(): jnp.dot(flat, joined, preferred_element_type=jnp.float32)  8.6 us
    unnamed x1, blocking collectives  6.94 us
    ppermute x2, starting transfers between devices, padded_2(): lax.ppermute(lax.slice_in_dim(block, block.shape[dim] - width, None, axis...  6.01 us
  transfers between devices with their start and end apart: 9, of which 4 were waited for; matrix products, arithmetic and copies ran while one was open for 8% of the time, Pallas kernels for 0%

profile of v1, /device:TPU:9, one launch (start us, length us, event | category | flops | bytes accessed | tf_op | source)
XLA Modules:
  0.0 142.9 jit_solution(8139991736967778958)
XLA Ops:
  0.0 1.2 fusion.9
  1.6 5.7 %all-reduce.18 = (f32[32]{0:T(128)S(1)}, f32[32]{0:T(128)S(1)}) all-reduce(f32[32]{0:T(128)S(1)} %reduce_sum.37, f32[32]{0:T(128)S(1)} %reduce_sum.39), channel_id=1, replica_groups=mesh['tm'=4,'ha'=2,'wa'=4] {'wa'}, use_global_device_ids=true, to_apply=%region_2.0 | all-reduce | flops 64 | bytes 512 | tf_op jit(solution)/shard_map/psum | solution.py:107
  7.3 3.8 %all-reduce.20 = (f32[32]{0:T(128)S(1)}, f32[32]{0:T(128)S(1)}) all-reduce(f32[32]{0:T(128)S(1)} %get-tuple-element.103, f32[32]{0:T(128)S(1)} %get-tuple-element.104), channel_id=1, replica_groups=mesh['tm'=4,'ha'=2,'wa'=4] {'ha'}, use_global_device_ids=true, to_apply=%region_3.0 | all-reduce | flops 64 | bytes 512 | tf_op jit(solution)/shard_map/psum | solution.py:107
  13.3 6.9 %all-reduce.19 = (f32[128]{0:T(128)S(1)}, f32[128]{0:T(128)S(1)}) all-reduce(f32[128]{0:T(128)S(1)} %dynamic-update-slice.12, f32[128]{0:T(128)S(1)} %dynamic-update-slice.13), channel_id=2, replica_groups=mesh['tm'=4,'ha'=2,'wa'=4] {'tm'}, use_global_device_ids=true, to_apply=%add.16 | all-reduce | flops 256 | bytes 2048
  20.8 1.4 %fusion.18 = bf16[2,16,16,512]{3,2,1,0:T(8,128)(2,1)S(1)} fusion(bf16[2,16,16,512]{3,2,1,0:T(8,128)(2,1)} %param.17, f32[512]{0:T(512)} %param.19, f32[512]{0:T(512)} %param.18, f32[512]{0:T(512)S(1)} %mul.34, f32[512]{0:T(512)S(1)} %sub.13), kind=kLoop, calls=%fused_computation.42 | loop fusion | flops 2621440 | bytes 1056768 | tf_op jit(solution)/shard_map/convert_element_type | solution.py:125
  22.2 1.3 collective-permute-start.1
  23.5 4.0 %collective-permute-start = (bf16[2,1,16,512]{3,2,1,0:T(8,128)(2,1)S(1)}, bf16[2,1,16,512]{3,2,1,0:T(8,128)(2,1)S(1)}, u32[]{:S(2)}, u32[]{:S(2)}) collective-permute-start(bf16[2,1,16,512]{3,2,1,0:T(8,128)(2,1)S(1)} %get-tuple-element.189), channel_id=1, source_target_pairs={{0,4},{1,5},{2,6},{3,7},{8,12},{9,13},{10,14},{11,15},{16,20},{17,... | collective-permute-start | bytes 98312 | tf_op jit(solution)/shard_map/ppermute | solution.py:27
  27.5 5.9 %fusion.58 = (bf16[1,1,3,512,256]{4,3,2,1,0:T(8,128)(2,1)S(1)}, bf16[1,1,3,512,256]{4,3,2,1,0:T(8,128)(2,1)}, bf16[1,1,3,512,256]{4,3,2,1,0:T(8,128)(2,1)}, bf16...) fusion(bf16[3,3,3,512,256]{4,3,2,1,0:T(8,128)(2,1)} %param.20), kind=kLoop, calls=%fused_computation.136 | loop fusion | bytes 14155776 | tf_op jit(solution)/shard_map/slice | solution.py:66
  33.6 7.5 %collective-permute-start.3 = (bf16[2,18,1,512]{3,2,1,0:T(2,128)(2,1)S(1)}, bf16[2,18,1,512]{3,2,1,0:T(2,128)(2,1)S(1)}, u32[]{:S(2)}, u32[]{:S(2)}) collective-permute-start(bf16[2,18,1,512]{3,2,1,0:T(2,128)(2,1)S(1)} %get-tuple-element.185), channel_id=1, source_target_pairs={{1,0},{2,1},{3,2},{5,4},{6,5},{7,6},{9,8},{10,9},{11,10},{13,12},{... | collective-permute-start | bytes 110600 | tf_op jit(solution)/shard_map/ppermute | solution.py:30
  41.1 2.0 %collective-permute-start.2 = (bf16[2,18,1,512]{3,2,1,0:T(2,128)(2,1)S(1)}, bf16[2,18,1,512]{3,2,1,0:T(2,128)(2,1)S(1)}, u32[]{:S(2)}, u32[]{:S(2)}) collective-permute-start(bf16[2,18,1,512]{3,2,1,0:T(2,128)(2,1)S(1)} %get-tuple-element.184), channel_id=1, source_target_pairs={{0,1},{1,2},{2,3},{4,5},{5,6},{6,7},{8,9},{9,10},{10,11},{12,13},{... | collective-permute-start | bytes 110600 | tf_op jit(solution)/shard_map/ppermute | solution.py:27
  45.1 3.2 %collective-permute-start.4 = (bf16[2,18,18,512]{3,2,1,0:T(8,128)(2,1)S(1)}, bf16[2,18,18,512]{3,2,1,0:T(8,128)(2,1)S(1)}, u32[]{:S(2)}, u32[]{:S(2)}) collective-permute-start(bf16[2,18,18,512]{3,2,1,0:T(8,128)(2,1)S(1)} %pad_maximum_fusion.10), channel_id=1, source_target_pairs={{0,8},{8,16},{16,24},{1,9},{9,17},{17,25},{2,10},{10,18},{18,26},{... | collective-permute-start | bytes 1990664 | tf_op jit(solution)/shard_map/ppermute | solution.py:38
  51.6 17.7 %collective-permute-done.4 = bf16[2,18,18,512]{3,2,1,0:T(8,128)(2,1)S(1)} collective-permute-done((bf16[2,18,18,512]{3,2,1,0:T(8,128)(2,1)S(1)}, bf16[2,18,18,512]{3,2,1,0:T(8,128)(2,1)S(1)}, u32[]{:S(2)}, u32[]{:S(2)}) %collective-permute-start.4) | collective-permute-done | bytes 663584 | tf_op jit(solution)/shard_map/ppermute | solution.py:38
  80.5 1.8 %fusion.43 = f32[512,1024]{1,0:T(8,128)} fusion(bf16[512,256]{1,0:T(8,128)(2,1)S(1)} %fusion.8, bf16[256,256]{1,0:T(8,128)(2,1)S(1)} %copy-done.30, bf16[256,256]{1,0:T(8,128)(2,1)S(1)} %copy-done.31, bf16[256,256]{1,0:T(8,128)(2,1)S(1)} %get-tuple-element.127, bf16[256,256]{1,0:T(8,128)(2,1)S(1)} %get-tuple-element.128), kind=kOutput, calls=%fused_computation.75 | convolution fusion | flops 270532608 | bytes 2883584 | tf_op jit(solution)/shard_map/dot_general | solution.py:88
  82.3 2.2 %reshape.235 = f32[2,16,16,4,256]{4,3,2,1,0:T(4,128)S(1)} reshape(f32[512,1024]{1,0:T(8,128)} %fusion.43) | data formatting | bytes 4194304 | tf_op jit(solution)/shard_map/reshape | solution.py:88
  84.5 1.9 %fusion.62 = (f32[2,16,16,1,256]{4,3,2,1,0:T(1,128)S(1)}, f32[2,16,16,1,256]{4,3,2,1,0:T(1,128)S(1)}, f32[2,16,16,1,256]{4,3,2,1,0:T(1,128)S(1)}, f32[2,16,16,1,256]{4,3,2,1,0:T(1,128)S(1)}) fusion(f32[2,16,16,4,256]{4,3,2,1,0:T(4,128)S(1)} %reshape.235), kind=kLoop, calls=%fused_computation.140 | loop fusion | bytes 4194304 | tf_op jit(solution)/shard_map/slice | solution.py:95
  88.2 1.8 %fusion.35 = f32[512,1024]{1,0:T(8,128)} fusion(bf16[512,256]{1,0:T(8,128)(2,1)S(1)} %fusion.8, bf16[256,256]{1,0:T(8,128)(2,1)S(1)} %copy-done.26, bf16[256,256]{1,0:T(8,128)(2,1)S(1)} %copy-done.27, bf16[256,256]{1,0:T(8,128)(2,1)S(1)} %copy-done.28, bf16[256,256]{1,0:T(8,128)(2,1)S(1)} %copy-done.29), kind=kOutput, calls=%fused_computation.67 | convolution fusion | flops 270532608 | bytes 2883584 | tf_op jit(solution)/shard_map/dot_general | solution.py:88
  90.0 2.2 %reshape.234 = f32[2,16,16,4,256]{4,3,2,1,0:T(4,128)S(1)} reshape(f32[512,1024]{1,0:T(8,128)} %fusion.35) | data formatting | bytes 4194304 | tf_op jit(solution)/shard_map/reshape | solution.py:88
  92.2 1.9 %fusion.61 = (f32[2,16,16,1,256]{4,3,2,1,0:T(1,128)S(1)}, f32[2,16,16,1,256]{4,3,2,1,0:T(1,128)S(1)}, f32[2,16,16,1,256]{4,3,2,1,0:T(1,128)S(1)}, f32[2,16,16,1,256]{4,3,2,1,0:T(1,128)S(1)}) fusion(f32[2,16,16,4,256]{4,3,2,1,0:T(4,128)S(1)} %reshape.234), kind=kLoop, calls=%fused_computation.139 | loop fusion | bytes 4194304 | tf_op jit(solution)/shard_map/slice | solution.py:95
  97.5 1.8 %fusion.27 = f32[512,1024]{1,0:T(8,128)} fusion(bf16[512,256]{1,0:T(8,128)(2,1)S(1)} %fusion.8, bf16[256,256]{1,0:T(8,128)(2,1)S(1)} %copy-done.22, bf16[256,256]{1,0:T(8,128)(2,1)S(1)} %copy-done.23, bf16[256,256]{1,0:T(8,128)(2,1)S(1)} %copy-done.24, bf16[256,256]{1,0:T(8,128)(2,1)S(1)} %copy-done.25), kind=kOutput, calls=%fused_computation.59 | convolution fusion | flops 270532608 | bytes 2883584 | tf_op jit(solution)/shard_map/dot_general | solution.py:88
  99.3 2.2 %reshape.233 = f32[2,16,16,4,256]{4,3,2,1,0:T(4,128)S(1)} reshape(f32[512,1024]{1,0:T(8,128)} %fusion.27) | data formatting | bytes 4194304 | tf_op jit(solution)/shard_map/reshape | solution.py:88
  101.5 1.9 %fusion.60 = (f32[2,16,16,1,256]{4,3,2,1,0:T(1,128)S(1)}, f32[2,16,16,1,256]{4,3,2,1,0:T(1,128)S(1)}, f32[2,16,16,1,256]{4,3,2,1,0:T(1,128)S(1)}, f32[2,16,16,1,256]{4,3,2,1,0:T(1,128)S(1)}) fusion(f32[2,16,16,4,256]{4,3,2,1,0:T(4,128)S(1)} %reshape.233), kind=kLoop, calls=%fused_computation.138 | loop fusion | bytes 4194304 | tf_op jit(solution)/shard_map/slice | solution.py:95
  107.3 2.0 %reshape.232 = f32[2,16,16,4,256]{4,3,2,1,0:T(4,128)} reshape(f32[512,1024]{1,0:T(8,128)S(1)} %fusion.19) | data formatting | bytes 4194304 | tf_op jit(solution)/shard_map/reshape | solution.py:88
  109.3 5.9 %fusion.59 = (f32[2,16,16,1,256]{4,3,2,1,0:T(1,128)S(1)}, f32[2,16,16,1,256]{4,3,2,1,0:T(1,128)S(1)}, f32[2,16,16,1,256]{4,3,2,1,0:T(1,128)S(1)}, f32[2,16,16,1,256]{4,3,2,1,0:T(1,128)S(1)}) fusion(f32[2,16,16,4,256]{4,3,2,1,0:T(4,128)} %reshape.232), kind=kLoop, calls=%fused_computation.137 | loop fusion | bytes 4194304 | tf_op jit(solution)/shard_map/slice | solution.py:95
  120.0 1.2 copy.43
  122.1 1.3 collective-permute-start.5
  124.2 1.3 collective-permute-start.6
  126.0 2.9 %collective-permute-done.6 = bf16[2,34,256]{2,0,1:T(2,128)(2,1)S(1)} collective-permute-done((bf16[2,34,256]{2,0,1:T(2,128)(2,1)S(1)}, bf16[2,34,256]{2,0,1:T(2,128)(2,1)S(1)}, u32[]{:S(2)}, u32[]{:S(2)}) %collective-permute-start.6) | collective-permute-done | bytes 34848 | tf_op jit(solution)/shard_map/ppermute | solution.py:38
  129.0 2.8 %scatter-add.15 = f32[2,32,34,256]{3,1,0,2:T(8,128)S(1)} dynamic-update-slice(f32[2,32,34,256]{3,1,0,2:T(8,128)S(1)} %copy.45, f32[2,1,34,256]{3,1,0,2:T(1,128)S(1)} %copy_add_fusion, s32[]{:T(128)} %constant.128.clone.1, s32[]{:T(128)} %constant.134.clone.1, s32[]{:T(128)} %constant.128.clone.1, s32[]{:T(128)} %constant.128.clone.1) | dynamic-update-slice | bytes 139268 | tf_op jit(solution)/shard_map/scatter-add | solution.py:143
  132.0 3.6 %collective-permute-start.7 = (bf16[2,32,256]{2,1,0:T(8,128)(2,1)S(1)}, bf16[2,32,256]{2,1,0:T(8,128)(2,1)S(1)}, u32[]{:S(2)}, u32[]{:S(2)}) collective-permute-start(bf16[2,32,256]{2,1,0:T(8,128)(2,1)S(1)} %get-tuple-element.166), channel_id=1, source_target_pairs={{0,1},{1,2},{2,3},{4,5},{5,6},{6,7},{8,9},{9,10},{10,11},{12,13},{... | collective-permute-start | bytes 98312 | tf_op jit(solution)/shard_map/ppermute | solution.py:38
  135.8 1.9 %collective-permute-start.8 = (bf16[2,32,256]{2,1,0:T(8,128)(2,1)S(1)}, bf16[2,32,256]{2,1,0:T(8,128)(2,1)S(1)}, u32[]{:S(2)}, u32[]{:S(2)}) collective-permute-start(bf16[2,32,256]{2,1,0:T(8,128)(2,1)S(1)} %get-tuple-element.165), channel_id=1, source_target_pairs={{1,0},{2,1},{3,2},{5,4},{6,5},{7,6},{9,8},{10,9},{11,10},{13,12},{... | collective-permute-start | bytes 98312 | tf_op jit(solution)/shard_map/ppermute | solution.py:38
  137.8 3.3 %collective-permute-done.8 = bf16[2,32,256]{2,1,0:T(8,128)(2,1)S(1)} collective-permute-done((bf16[2,32,256]{2,1,0:T(8,128)(2,1)S(1)}, bf16[2,32,256]{2,1,0:T(8,128)(2,1)S(1)}, u32[]{:S(2)}, u32[]{:S(2)}) %collective-permute-start.8) | collective-permute-done | bytes 32800 | tf_op jit(solution)/shard_map/ppermute | solution.py:38
  141.4 1.6 %copy.46 = bf16[2,32,32,256]{3,2,1,0:T(8,128)(2,1)} copy(bf16[2,32,32,256]{3,1,0,2:T(8,128)(2,1)S(1)} %add_convert_fusion) | data formatting | bytes 2097152 | tf_op jit(solution)/shard_map/convert_element_type | solution.py:149
  (157 shorter events, 35.2 us)
Async XLA Ops:
  22.2 11.2 %collective-permute-start.1 = (bf16[2,1,16,512]{3,2,1,0:T(8,128)(2,1)S(1)}, bf16[2,1,16,512]{3,2,1,0:T(8,128)(2,1)S(1)}, u32[]{:S(2)}, u32[]{:S(2)}) collective-permute-start(bf16[2,1,16,512]{3,2,1,0:T(8,128)(2,1)S(1)} %get-tuple-element.190), channel_id=1, source_target_pairs={{4,0},{5,1},{6,2},{7,3},{12,8},{13,9},{14,10},{15,11},{20,16},{21,... | collective-permute-start | bytes 98312 | tf_op jit(solution)/shard_map/ppermute | solution.py:30
  23.5 9.9 %collective-permute-start = (bf16[2,1,16,512]{3,2,1,0:T(8,128)(2,1)S(1)}, bf16[2,1,16,512]{3,2,1,0:T(8,128)(2,1)S(1)}, u32[]{:S(2)}, u32[]{:S(2)}) collective-permute-start(bf16[2,1,16,512]{3,2,1,0:T(8,128)(2,1)S(1)} %get-tuple-element.189), channel_id=1, source_target_pairs={{0,4},{1,5},{2,6},{3,7},{8,12},{9,13},{10,14},{11,15},{16,20},{17,... | collective-permute-start | bytes 98312 | tf_op jit(solution)/shard_map/ppermute | solution.py:27
  27.5 15.6 %copy-start.8 = (bf16[4,4,256,256]{3,2,1,0:T(8,128)(2,1)S(1)}, bf16[4,4,256,256]{3,2,1,0:T(8,128)(2,1)}, u32[]{:S(2)}) copy-start(bf16[4,4,256,256]{3,2,1,0:T(8,128)(2,1)} %param.22) | copy-start | bytes 6291460
  33.6 10.8 %collective-permute-start.3 = (bf16[2,18,1,512]{3,2,1,0:T(2,128)(2,1)S(1)}, bf16[2,18,1,512]{3,2,1,0:T(2,128)(2,1)S(1)}, u32[]{:S(2)}, u32[]{:S(2)}) collective-permute-start(bf16[2,18,1,512]{3,2,1,0:T(2,128)(2,1)S(1)} %get-tuple-element.185), channel_id=1, source_target_pairs={{1,0},{2,1},{3,2},{5,4},{6,5},{7,6},{9,8},{10,9},{11,10},{13,12},{... | collective-permute-start | bytes 110600 | tf_op jit(solution)/shard_map/ppermute | solution.py:30
  41.1 3.4 %collective-permute-start.2 = (bf16[2,18,1,512]{3,2,1,0:T(2,128)(2,1)S(1)}, bf16[2,18,1,512]{3,2,1,0:T(2,128)(2,1)S(1)}, u32[]{:S(2)}, u32[]{:S(2)}) collective-permute-start(bf16[2,18,1,512]{3,2,1,0:T(2,128)(2,1)S(1)} %get-tuple-element.184), channel_id=1, source_target_pairs={{0,1},{1,2},{2,3},{4,5},{5,6},{6,7},{8,9},{9,10},{10,11},{12,13},{... | collective-permute-start | bytes 110600 | tf_op jit(solution)/shard_map/ppermute | solution.py:27
  45.1 24.3 %collective-permute-start.4 = (bf16[2,18,18,512]{3,2,1,0:T(8,128)(2,1)S(1)}, bf16[2,18,18,512]{3,2,1,0:T(8,128)(2,1)S(1)}, u32[]{:S(2)}, u32[]{:S(2)}) collective-permute-start(bf16[2,18,18,512]{3,2,1,0:T(8,128)(2,1)S(1)} %pad_maximum_fusion.10), channel_id=1, source_target_pairs={{0,8},{8,16},{16,24},{1,9},{9,17},{17,25},{2,10},{10,18},{18,26},{... | collective-permute-start | bytes 1990664 | tf_op jit(solution)/shard_map/ppermute | solution.py:38
  49.8 1.2 copy-start.2
  73.4 1.4 copy-start.7
  75.5 1.6 %copy-start.5 = (bf16[1,1,3,512,256]{4,3,2,1,0:T(8,128)(2,1)S(1)}, bf16[1,1,3,512,256]{4,3,2,1,0:T(8,128)(2,1)}, u32[]{:S(2)}) copy-start(bf16[1,1,3,512,256]{4,3,2,1,0:T(8,128)(2,1)} %get-tuple-element.116) | copy-start | bytes 2359300
  86.5 1.8 %copy-start.26 = (bf16[256,256]{1,0:T(8,128)(2,1)S(1)}, bf16[256,256]{1,0:T(8,128)(2,1)}, u32[]{:S(2)}) copy-start(bf16[256,256]{1,0:T(8,128)(2,1)} %get-tuple-element.129) | copy-start | bytes 393220
  86.5 1.7 %copy-start.27 = (bf16[256,256]{1,0:T(8,128)(2,1)S(1)}, bf16[256,256]{1,0:T(8,128)(2,1)}, u32[]{:S(2)}) copy-start(bf16[256,256]{1,0:T(8,128)(2,1)} %get-tuple-element.130) | copy-start | bytes 393220
  86.5 1.7 %copy-start.28 = (bf16[256,256]{1,0:T(8,128)(2,1)S(1)}, bf16[256,256]{1,0:T(8,128)(2,1)}, u32[]{:S(2)}) copy-start(bf16[256,256]{1,0:T(8,128)(2,1)} %get-tuple-element.131) | copy-start | bytes 393220
  86.5 1.7 %copy-start.29 = (bf16[256,256]{1,0:T(8,128)(2,1)S(1)}, bf16[256,256]{1,0:T(8,128)(2,1)}, u32[]{:S(2)}) copy-start(bf16[256,256]{1,0:T(8,128)(2,1)} %get-tuple-element.132) | copy-start | bytes 393220
  95.0 2.5 %copy-start.22 = (bf16[256,256]{1,0:T(8,128)(2,1)S(1)}, bf16[256,256]{1,0:T(8,128)(2,1)}, u32[]{:S(2)}) copy-start(bf16[256,256]{1,0:T(8,128)(2,1)} %get-tuple-element.133) | copy-start | bytes 393220
  95.0 2.5 %copy-start.23 = (bf16[256,256]{1,0:T(8,128)(2,1)S(1)}, bf16[256,256]{1,0:T(8,128)(2,1)}, u32[]{:S(2)}) copy-start(bf16[256,256]{1,0:T(8,128)(2,1)} %get-tuple-element.134) | copy-start | bytes 393220
  95.0 2.5 %copy-start.24 = (bf16[256,256]{1,0:T(8,128)(2,1)S(1)}, bf16[256,256]{1,0:T(8,128)(2,1)}, u32[]{:S(2)}) copy-start(bf16[256,256]{1,0:T(8,128)(2,1)} %get-tuple-element.135) | copy-start | bytes 393220
  95.0 2.5 %copy-start.25 = (bf16[256,256]{1,0:T(8,128)(2,1)S(1)}, bf16[256,256]{1,0:T(8,128)(2,1)}, u32[]{:S(2)}) copy-start(bf16[256,256]{1,0:T(8,128)(2,1)} %get-tuple-element.136) | copy-start | bytes 393220
  104.3 2.5 %copy-start.19 = (bf16[256,256]{1,0:T(8,128)(2,1)S(1)}, bf16[256,256]{1,0:T(8,128)(2,1)}, u32[]{:S(2)}) copy-start(bf16[256,256]{1,0:T(8,128)(2,1)} %get-tuple-element.137) | copy-start | bytes 393220
  104.3 2.5 %copy-start.20 = (bf16[256,256]{1,0:T(8,128)(2,1)S(1)}, bf16[256,256]{1,0:T(8,128)(2,1)}, u32[]{:S(2)}) copy-start(bf16[256,256]{1,0:T(8,128)(2,1)} %get-tuple-element.138) | copy-start | bytes 393220
  104.3 2.5 %copy-start.21 = (bf16[256,256]{1,0:T(8,128)(2,1)S(1)}, bf16[256,256]{1,0:T(8,128)(2,1)}, u32[]{:S(2)}) copy-start(bf16[256,256]{1,0:T(8,128)(2,1)} %get-tuple-element.139) | copy-start | bytes 393220
  115.2 1.2 copy-start.10
  115.3 1.4 copy-start.11
  115.3 1.4 copy-start.12
  115.4 1.6 %copy-start.13 = (f32[2,16,16,1,256]{4,2,1,0,3:T(8,128)S(1)}, f32[2,16,16,1,256]{4,2,1,0,3:T(8,128)}, u32[]{:S(2)}) copy-start(f32[2,16,16,1,256]{4,2,1,0,3:T(8,128)} %copy.86) | copy-start | bytes 1572868
  115.4 1.7 %copy-start.14 = (f32[2,16,16,1,256]{4,2,1,0,3:T(8,128)S(1)}, f32[2,16,16,1,256]{4,2,1,0,3:T(8,128)}, u32[]{:S(2)}) copy-start(f32[2,16,16,1,256]{4,2,1,0,3:T(8,128)} %copy.87) | copy-start | bytes 1572868
  117.4 1.3 copy-start.17
  117.4 1.5 %copy-start.18 = (f32[2,16,16,1,256]{4,2,1,0,3:T(8,128)S(1)}, f32[2,16,16,1,256]{4,2,1,0,3:T(8,128)}, u32[]{:S(2)}) copy-start(f32[2,16,16,1,256]{4,2,1,0,3:T(8,128)} %copy.91) | copy-start | bytes 1572868
  122.1 3.4 %collective-permute-start.5 = (bf16[2,34,256]{2,0,1:T(2,128)(2,1)S(1)}, bf16[2,34,256]{2,0,1:T(2,128)(2,1)S(1)}, u32[]{:S(2)}, u32[]{:S(2)}) collective-permute-start(bf16[2,34,256]{2,0,1:T(2,128)(2,1)S(1)} %get-tuple-element.164), channel_id=1, source_target_pairs={{0,4},{1,5},{2,6},{3,7},{8,12},{9,13},{10,14},{11,15},{16,20},{17,... | collective-permute-start | bytes 104456 | tf_op jit(solution)/shard_map/ppermute | solution.py:38
  124.2 4.7 %collective-permute-start.6 = (bf16[2,34,256]{2,0,1:T(2,128)(2,1)S(1)}, bf16[2,34,256]{2,0,1:T(2,128)(2,1)S(1)}, u32[]{:S(2)}, u32[]{:S(2)}) collective-permute-start(bf16[2,34,256]{2,0,1:T(2,128)(2,1)S(1)} %get-tuple-element.163), channel_id=1, source_target_pairs={{4,0},{5,1},{6,2},{7,3},{12,8},{13,9},{14,10},{15,11},{20,16},{21,... | collective-permute-start | bytes 104456 | tf_op jit(solution)/shard_map/ppermute | solution.py:38
  132.0 9.0 %copy-start.33 = (f32[256]{0:T(256)S(1)}, f32[256]{0:T(256)}, u32[]{:S(2)}) copy-start(f32[256]{0:T(256)} %param.23) | copy-start | bytes 3076
  132.0 5.7 %collective-permute-start.7 = (bf16[2,32,256]{2,1,0:T(8,128)(2,1)S(1)}, bf16[2,32,256]{2,1,0:T(8,128)(2,1)S(1)}, u32[]{:S(2)}, u32[]{:S(2)}) collective-permute-start(bf16[2,32,256]{2,1,0:T(8,128)(2,1)S(1)} %get-tuple-element.166), channel_id=1, source_target_pairs={{0,1},{1,2},{2,3},{4,5},{5,6},{6,7},{8,9},{9,10},{10,11},{12,13},{... | collective-permute-start | bytes 98312 | tf_op jit(solution)/shard_map/ppermute | solution.py:38
  135.8 5.2 %collective-permute-start.8 = (bf16[2,32,256]{2,1,0:T(8,128)(2,1)S(1)}, bf16[2,32,256]{2,1,0:T(8,128)(2,1)S(1)}, u32[]{:S(2)}, u32[]{:S(2)}) collective-permute-start(bf16[2,32,256]{2,1,0:T(8,128)(2,1)S(1)} %get-tuple-element.165), channel_id=1, source_target_pairs={{1,0},{2,1},{3,2},{5,4},{6,5},{7,6},{9,8},{10,9},{11,10},{13,12},{... | collective-permute-start | bytes 98312 | tf_op jit(solution)/shard_map/ppermute | solution.py:38
  (11 other events, 11.5 us)
